TPU v7x, 256 devices: a whole 4x4x8 slice. The times are simulated.
256 devices in a mesh: dp: 32 (over z, x), tensor: 8 (over y, core).
Axes of the slice: x: 4, y: 4, z: 8, core: 2. Of those that a mesh axis runs over, the one named last changes fastest.
Arguments:
- activations: bfloat16 [28672, 4096], P('dp', 'tensor'), may hold values from -6 to 6
- out_grads: bfloat16 [28672, 4096], P('dp', 'tensor'), may hold values from -6 to 6
- gate_act: bfloat16 [28672, 14336], P('dp', 'tensor'), may hold values from -6 to 6
- w_down: bfloat16 [14336, 4096], P('tensor', 'dp'), may hold values from -0.09375 to 0.09375
- proj_in: bfloat16 [4096, 64], P('tensor'), may hold values from -0.09375 to 0.09375
- proj_out: bfloat16 [14336, 64], P('tensor'), may hold values from -0.046875 to 0.046875
- lengths: int32 [32, 8], P('dp'), may hold values from 1 to 448, 896 in all within a row
- assign: int32 [256], replicated, may hold values from 0 to 255, each once
Outputs:
- loggrads: float32 [256, 64, 64], P('dp', 'tensor')
Inputs may be any that keep to these rules, and one draw needn't show every extreme that they name: `lengths`: each row gives the token counts of the 8 sequences packed into one data group's 896 rows and sums to 896. `assign`: a permutation of the sequence numbers.
All inputs are finite; a program needn't handle non-finite values.
Results may differ from a plain program's by a relative error of at most 0.013.
Values may be sent and summed in bfloat16 or wider, within the bound.
No kernel may reach another device: no remote copies, remote signals or barrier semaphores. Data moves between devices by JAX's collectives and lax.ppermute only.
A program may use at most 128 MiB of HBM per device.

v0:
```python
import jax
import jax.numpy as jnp
from jax import lax
from jax.sharding import PartitionSpec as P


def shards(activations, out_grads, gate_act, w_down, proj_in, proj_out, lengths, assign):
    tok_rows = activations.shape[0]
    rank_all = proj_in.shape[1]
    full_grads = lax.all_gather(out_grads, "tensor", axis=1, tiled=True)
    hidden_grad = lax.dot_general(
        full_grads,
        lax.all_gather(w_down, "dp", axis=1, tiled=True),
        (((1,), (1,)), ((), ())),
        preferred_element_type=jnp.float32,
    )
    up_grad = (hidden_grad * gate_act.astype(jnp.float32)).astype(jnp.bfloat16)
    out_part = jnp.dot(up_grad, proj_out, preferred_element_type=jnp.float32)
    in_part = jnp.dot(activations, proj_in, preferred_element_type=jnp.float32)
    col_count = rank_all // lax.axis_size("tensor")
    shard_index = lax.axis_index("tensor")
    in_sum, out_sum = lax.psum((in_part, out_part), "tensor")
    in_mine = lax.dynamic_slice_in_dim(in_sum, shard_index * col_count, col_count, 1)
    seq_lengths = lengths[0]
    seq_ends = jnp.cumsum(seq_lengths)
    starts = seq_ends - seq_lengths
    positions = lax.iota(jnp.int32, tok_rows)
    inside = (positions[None, :] >= starts[:, None]) & (positions[None, :] < seq_ends[:, None])
    member = jnp.where(inside, 1.0 / seq_lengths[:, None].astype(jnp.float32), 0.0)
    weighted = member[:, :, None] * in_mine[None, :, :]
    result = jnp.einsum("ctp,tq->cpq", weighted, out_sum, precision=lax.Precision.HIGHEST)
    per_group = seq_lengths.shape[0]
    group_count = lax.axis_size("dp")
    seq_total = per_group * group_count
    group_index = lax.axis_index("dp")
    mine_ids = lax.dynamic_slice_in_dim(assign, group_index * per_group, per_group, 0)
    placing = (mine_ids[None, :] == lax.iota(jnp.int32, seq_total)[:, None]).astype(jnp.float32)
    flat_result = result.reshape(per_group, col_count * rank_all)
    spread = jnp.dot(placing, flat_result, precision=lax.Precision.HIGHEST)
    owned = lax.psum_scatter(
        spread.astype(jnp.bfloat16), "dp", scatter_dimension=0, tiled=True
    ).astype(jnp.float32)
    return owned.reshape(per_group, col_count, rank_all)


def solution(mesh):
    in_specs = (
        P("dp", "tensor"),
        P("dp", "tensor"),
        P("dp", "tensor"),
        P("tensor", "dp"),
        P("tensor", None),
        P("tensor", None),
        P("dp", None),
        P(),
    )
    out_specs = P("dp", "tensor", None)
    return jax.shard_map(shards, mesh=mesh, in_specs=in_specs, out_specs=out_specs, check_vma=False)
```

profile of v0, /device:TPU:8, one launch (start us, length us, event | category | flops | bytes accessed | tf_op | source)
XLA Modules:
  0.0 511.5 jit_solution(17634856475808253684)
XLA Ops:
  6.5 0.0 copy-start
  6.5 0.0 all-gather.3.cloned.1.call-start
  6.5 0.7 all-gather.3.cloned.1.call-update
  7.3 0.0 all-gather.5.cloned.1.call-start
  7.3 0.7 all-gather.5.cloned.1.call-update
  8.0 0.0 all-reduce.3.cloned.1.call-start
  8.1 0.8 reduce-window.7
  8.9 0.7 bitcast_subtract_fusion
  9.5 0.0 copy-done
  9.5 2.0 fusion.10
  11.5 0.0 copy-start.2
  11.5 0.0 copy-start.1
  11.5 47.6 %all-gather.3.cloned.1.call-done = bf16[896,4096]{1,0:T(8,128)(2,1)} async-done(((bf16[896,512]{1,0:T(8,128)(2,1)}), bf16[896,4096]{1,0:T(8,128)(2,1)}) %all-gather.3.cloned.1.call-update) | async-done | bytes 7340048 | tf_op jit(solution)/shard_map/all_gather | solution.py:10
  59.1 142.3 %all-gather.5.cloned.1.call-done = bf16[1792,4096]{1,0:T(8,128)(2,1)} async-done(((bf16[1792,128]{1,0:T(8,128)(2,1)}), bf16[1792,4096]{1,0:T(8,128)(2,1)}) %all-gather.5.cloned.1.call-update) | async-done | bytes 14680080 | tf_op jit(solution)/shard_map/all_gather | solution.py:13
  201.4 23.2 %fusion = f32[896,64]{0,1:T(8,128)} fusion(bf16[1792,64]{0,1:T(8,128)(2,1)} %param.13, bf16[896,1792]{1,0:T(8,128)(2,1)} %param.10, bf16[896,4096]{1,0:T(8,128)(2,1)} %all-gather.3.cloned.1.call-done, bf16[1792,4096]{1,0:T(8,128)(2,1)} %all-gather.5.cloned.1.call-done), kind=kOutput, calls=%fused_computation.1 | convolution fusion | flops 13363675136 | bytes 25690112 | tf_op jit(solution)/shard_map/dot_general | solution.py:18
  224.6 0.0 all-reduce.3.cloned.1.call-update
  224.7 0.0 reduce-scatter.2.cloned.1.call-start
  224.7 0.0 copy-done.2
  224.7 0.0 copy-done.1
  224.8 0.1 dynamic_slice.6
  224.8 0.1 fusion.8
  224.9 60.4 %all-reduce.3.cloned.1.call-done = (f32[896,64]{0,1:T(8,128)}, f32[896,64]{0,1:T(8,128)}) async-done(((f32[896,64]{0,1:T(8,128)}, f32[896,64]{0,1:T(8,128)}), (f32[896,64]{0,1:T(8,128)}, f32[896,64]{0,1:T(8,128)})) %all-reduce.3.cloned.1.call-update) | async-done | bytes 458768 | tf_op jit(solution)/shard_map/psum | solution.py:22
  285.3 0.8 constant_dynamic-slice_fusion
  286.1 1.3 fusion.1
  287.4 0.1 reshape.108
  287.5 1.0 convolution_convert_fusion
  288.5 0.0 reduce-scatter.2.cloned.1.call-update
  288.5 215.0 %reduce-scatter.2.cloned.1.call-done = bf16[8,512]{1,0:T(8,128)(2,1)} async-done(((bf16[256,512]{1,0:T(8,128)(2,1)}), bf16[8,512]{1,0:T(8,128)(2,1)}) %reduce-scatter.2.cloned.1.call-update) | async-done | bytes 8208 | tf_op jit(solution)/shard_map/reduce_scatter | solution.py:40
  503.6 1.4 reshape.112
  (1 shorter events, 0.0 us)
Async XLA Ops:
  6.5 3.0 copy-start
  6.5 52.6 %all-gather.3.cloned.1.call-start = ((), (), s32[]{:S(2)}) async-start(), calls=%async_computation.1 | async-start | bytes 8257536 | tf_op jit(solution)/shard_map/all_gather | solution.py:10
  7.3 194.2 %all-gather.5.cloned.1.call-start = ((), (), s32[]{:S(2)}) async-start(), calls=%async_computation.2 | async-start | bytes 15138816 | tf_op jit(solution)/shard_map/all_gather | solution.py:13
  8.0 277.3 %all-reduce.3.cloned.1.call-start = ((), (), s32[]{:S(2)}) async-start(), calls=%async_computation.4 | async-start | bytes 917504 | tf_op jit(solution)/shard_map/psum | solution.py:22
  11.5 213.2 %copy-start.2 = (s32[1,8]{1,0:T(1,128)S(1)}, s32[1,8]{1,0:T(1,128)}, u32[]{:S(2)}) copy-start(s32[1,8]{1,0:T(1,128)} %param.14) | copy-start | bytes 100
  11.5 213.2 %copy-start.1 = (s32[256]{0:T(256)S(1)}, s32[256]{0:T(256)}, u32[]{:S(2)}) copy-start(s32[256]{0:T(256)} %param.15) | copy-start | bytes 3076
  224.7 278.9 %reduce-scatter.2.cloned.1.call-start = ((), (), s32[]{:S(2)}) async-start(), calls=%async_computation.3 | async-start | bytes 270336 | tf_op jit(solution)/shard_map/reduce_scatter | solution.py:40
Sparse Core Ops, SparseCore 0:
  9.2 49.8 all-gather.2
  61.6 139.7 all-gather.4
  224.8 60.4 all-reduce.2
  289.5 214.0 reduce-scatter.1
where the time goes:
time: 512 us; the launch traced here: 511 us
  waiting for transfers between devices  467 us (91%)
  matrix products  27.5 us (5%)
  between operations  13.2 us (3%)
    reduce_scatter x1, waiting for transfers between devices, shards(): lax.psum_scatter(spread.astype(jnp.bfloat16), 'dp', scatter_dimension=0,...  215 us
    all_gather x1, waiting for transfers between devices, shards(): lax.all_gather(w_down, 'dp', axis=1, tiled=True)  142 us
    psum x1, waiting for transfers between devices, shards(): in_sum, out_sum = lax.psum((in_part, out_part), 'tensor')  60.4 us
    all_gather x1, waiting for transfers between devices, shards(): full_grads = lax.all_gather(out_grads, 'tensor', axis=1, tiled=True)  47.6 us
    dot_general x1, matrix products, shards(): out_part = jnp.dot(up_grad, proj_out, preferred_element_type=jnp.float32)  23.2 us
  transfers between devices with their start and end apart: 4, of which 4 were waited for; matrix products, arithmetic and copies ran while one was open for 1% of the time, Pallas kernels for 0%

commit v1 on v0

--- a/solution.py
+++ b/solution.py
@@ -4,10 +4,20 @@
 from jax.sharding import PartitionSpec as P
 
 
+def pass_along(value, name, along):
+    size = lax.axis_size(name)
+    held, blocks = (value, [value])
+    for _ in range(size - 1):
+        held = lax.ppermute(held, name, [(i, (i + 1) % size) for i in range(size)])
+        blocks.insert(0, held)
+    line = jnp.concatenate(blocks, axis=along)
+    return jnp.roll(line, (lax.axis_index(name) + 1) * value.shape[along], axis=along)
+
+
 def shards(activations, out_grads, gate_act, w_down, proj_in, proj_out, lengths, assign):
     tok_rows = activations.shape[0]
     rank_all = proj_in.shape[1]
-    full_grads = lax.all_gather(out_grads, "tensor", axis=1, tiled=True)
+    full_grads = pass_along(out_grads, "tensor", 1)
     hidden_grad = lax.dot_general(
         full_grads,
         lax.all_gather(w_down, "dp", axis=1, tiled=True),

time: 512 us -> 462 us (0.902)
  waiting for transfers between devices: 467 us -> 386 us
  local copies, waits for them, and re-layouts: 2.3 us -> 32.4 us
    all_gather x1, waiting for transfers between devices: 142 us -> 23.6 us  [shards(): lax.all_gather(w_down, 'dp', axis=1, tiled=True)]
    ppermute x0 -> x7, waiting for transfers between devices: none -> 86.4 us  [pass_along(): held = lax.ppermute(held, name, [(i, (i + 1) % size) for i in range(size)])]
    all_gather x1 -> x0, waiting for transfers between devices: 47.6 us -> none  [shards(): full_grads = lax.all_gather(out_grads, 'tensor', axis=1, tiled=True)]
    unnamed x6 -> x41, local copies, waits for them, and re-layouts: 0.01 us -> 29 us
  transfers between devices with their start and end apart: 4 -> 10, of which waited for: 4 -> 10; matrix products, arithmetic and copies ran while one was open for 1% -> 7% of each run, Pallas kernels for 0% -> 0%
where the time goes in v1:
time: 462 us; the launch traced here: 461 us
  waiting for transfers between devices  386 us (84%)
  local copies, waits for them, and re-layouts  32.4 us (7%)
  matrix products  27.3 us (6%)
  between operations  13.2 us (3%)
    reduce_scatter x1, waiting for transfers between devices, shards(): lax.psum_scatter(spread.astype(jnp.bfloat16), 'dp', scatter_dimension=0,...  215 us
    ppermute x7, waiting for transfers between devices, pass_along(): held = lax.ppermute(held, name, [(i, (i + 1) % size) for i in range(size)])  86.4 us
    psum x1, waiting for transfers between devices, shards(): in_sum, out_sum = lax.psum((in_part, out_part), 'tensor')  60.5 us
    unnamed x41, local copies, waits for them, and re-layouts  29 us
    all_gather x1, waiting for transfers between devices, shards(): lax.all_gather(w_down, 'dp', axis=1, tiled=True)  23.6 us
    dot_general x1, matrix products, shards(): out_part = jnp.dot(up_grad, proj_out, preferred_element_type=jnp.float32)  22.7 us
  transfers between devices with their start and end apart: 10, of which 10 were waited for; matrix products, arithmetic and copies ran while one was open for 7% of the time, Pallas kernels for 0%

profile of v1, /device:TPU:8, one launch (start us, length us, event | category | flops | bytes accessed | tf_op | source)
XLA Modules:
  0.0 461.1 jit_solution(4586262221011154526)
XLA Ops:
  6.5 0.0 copy-start
  6.5 0.0 all-gather.2.cloned.1.call-start
  6.5 0.7 all-gather.2.cloned.1.call-update
  7.3 0.0 all-reduce.3.cloned.1.call-start
  7.3 0.0 collective-permute-start
  7.3 13.0 %collective-permute-done = bf16[896,512]{1,0:T(8,128)(2,1)S(1)} collective-permute-done((bf16[896,512]{1,0:T(8,128)(2,1)}, bf16[896,512]{1,0:T(8,128)(2,1)S(1)}, u32[]{:S(2)}, u32[]{:S(2)}) %collective-permute-start) | collective-permute-done | bytes 917536 | tf_op jit(solution)/shard_map/ppermute | solution.py:11
  20.3 0.0 collective-permute-start.1
  20.4 12.8 %collective-permute-done.1 = bf16[896,512]{1,0:T(8,128)(2,1)S(1)} collective-permute-done((bf16[896,512]{1,0:T(8,128)(2,1)S(1)}, bf16[896,512]{1,0:T(8,128)(2,1)S(1)}, u32[]{:S(2)}, u32[]{:S(2)}) %collective-permute-start.1) | collective-permute-done | bytes 917536 | tf_op jit(solution)/shard_map/ppermute | solution.py:11
  33.2 1.0 copy-done.2
  34.2 0.0 collective-permute-start.2
  34.2 12.8 %collective-permute-done.2 = bf16[896,512]{1,0:T(8,128)(2,1)S(1)} collective-permute-done((bf16[896,512]{1,0:T(8,128)(2,1)S(1)}, bf16[896,512]{1,0:T(8,128)(2,1)S(1)}, u32[]{:S(2)}, u32[]{:S(2)}) %collective-permute-start.2) | collective-permute-done | bytes 917536 | tf_op jit(solution)/shard_map/ppermute | solution.py:11
  47.0 0.9 copy-done.4
  47.9 0.0 collective-permute-start.3
  47.9 12.8 %collective-permute-done.3 = bf16[896,512]{1,0:T(8,128)(2,1)S(1)} collective-permute-done((bf16[896,512]{1,0:T(8,128)(2,1)S(1)}, bf16[896,512]{1,0:T(8,128)(2,1)S(1)}, u32[]{:S(2)}, u32[]{:S(2)}) %collective-permute-start.3) | collective-permute-done | bytes 917536 | tf_op jit(solution)/shard_map/ppermute | solution.py:11
  60.7 0.9 copy-done.6
  61.7 0.0 collective-permute-start.4
  61.7 12.8 %collective-permute-done.4 = bf16[896,512]{1,0:T(8,128)(2,1)S(1)} collective-permute-done((bf16[896,512]{1,0:T(8,128)(2,1)S(1)}, bf16[896,512]{1,0:T(8,128)(2,1)S(1)}, u32[]{:S(2)}, u32[]{:S(2)}) %collective-permute-start.4) | collective-permute-done | bytes 917536 | tf_op jit(solution)/shard_map/ppermute | solution.py:11
  74.5 0.9 copy-done.8
  75.4 0.0 collective-permute-start.5
  75.4 12.9 %collective-permute-done.5 = bf16[896,512]{1,0:T(8,128)(2,1)} collective-permute-done((bf16[896,512]{1,0:T(8,128)(2,1)S(1)}, bf16[896,512]{1,0:T(8,128)(2,1)}, u32[]{:S(2)}, u32[]{:S(2)}) %collective-permute-start.5) | collective-permute-done | bytes 917536 | tf_op jit(solution)/shard_map/ppermute | solution.py:11
  88.4 0.0 collective-permute-start.6
  88.4 0.8 reduce-window.7
  89.2 0.8 bitcast_subtract_fusion
  90.0 0.0 copy-done
  90.0 2.2 fusion.18
  92.3 9.2 %collective-permute-done.6 = bf16[896,512]{1,0:T(8,128)(2,1)} collective-permute-done((bf16[896,512]{1,0:T(8,128)(2,1)}, bf16[896,512]{1,0:T(8,128)(2,1)}, u32[]{:S(2)}, u32[]{:S(2)}) %collective-permute-start.6) | collective-permute-done | bytes 917536 | tf_op jit(solution)/shard_map/ppermute | solution.py:11
  101.5 2.3 constant_dynamic-update-slice_fusion.15
  103.8 2.2 constant_dynamic-update-slice_fusion.14
  106.0 2.2 constant_dynamic-update-slice_fusion.13
  108.2 2.3 constant_dynamic-update-slice_fusion.12
  110.5 2.2 constant_dynamic-update-slice_fusion.11
  112.7 2.2 constant_dynamic-update-slice_fusion.10
  115.0 1.0 constant_dynamic-update-slice_fusion.9
  116.0 0.0 copy-done.1
  116.0 1.1 constant_dynamic-update-slice_fusion.8
  117.1 2.2 constant_dynamic-update-slice_fusion.7
  119.3 2.3 constant_dynamic-update-slice_fusion.6
  121.7 0.0 copy-done.9
  121.7 1.0 constant_dynamic-update-slice_fusion.5
  122.7 0.0 copy-done.7
  122.7 1.0 constant_dynamic-update-slice_fusion.4
  123.7 0.0 copy-done.5
  123.7 1.0 constant_dynamic-update-slice_fusion.3
  124.7 0.0 copy-done.3
  124.7 1.0 constant_dynamic-update-slice_fusion.2
  125.7 1.0 constant_dynamic-update-slice_fusion.1
  126.7 1.0 constant_dynamic-update-slice_fusion
  127.8 23.6 %all-gather.2.cloned.1.call-done = bf16[1792,4096]{1,0:T(8,128)(2,1)} async-done(((bf16[1792,128]{1,0:T(8,128)(2,1)}), bf16[1792,4096]{1,0:T(8,128)(2,1)}) %all-gather.2.cloned.1.call-update) | async-done | bytes 14680080 | tf_op jit(solution)/shard_map/all_gather | solution.py:23
  151.4 0.0 copy-done.10
  151.4 22.7 %fusion.5 = f32[896,64]{0,1:T(8,128)} fusion(bf16[1792,64]{0,1:T(8,128)(2,1)S(1)} %copy-done.10, bf16[896,1792]{1,0:T(8,128)(2,1)} %param.10, bf16[1792,4096]{1,0:T(8,128)(2,1)} %all-gather.2.cloned.1.call-done, bf16[896,8192]{1,0:T(8,128)(2,1)} %constant_dynamic-update-slice_fusion, s32[]{:T(128)S(6)} %select_n.31), kind=kOutput, calls=%fused_computation.3 | convolution fusion | flops 13363675136 | bytes 25690116 | tf_op jit(solution)/shard_map/dot_general | solution.py:28
  174.1 0.0 all-reduce.3.cloned.1.call-update
  174.1 0.0 reduce-scatter.2.cloned.1.call-start
  174.2 0.0 copy-done.12
  174.2 0.0 copy-done.11
  174.2 0.1 dynamic_slice.10
  174.3 0.1 fusion.14
  174.3 60.5 %all-reduce.3.cloned.1.call-done = (f32[896,64]{0,1:T(8,128)}, f32[896,64]{0,1:T(8,128)}) async-done(((f32[896,64]{0,1:T(8,128)}, f32[896,64]{0,1:T(8,128)}), (f32[896,64]{0,1:T(8,128)}, f32[896,64]{0,1:T(8,128)})) %all-reduce.3.cloned.1.call-update) | async-done | bytes 458768 | tf_op jit(solution)/shard_map/psum | solution.py:32
  234.9 0.8 constant_dynamic-slice_fusion
  235.6 1.3 fusion.7
  236.9 0.1 reshape.108
  237.0 1.0 convolution_convert_fusion
  238.0 0.0 reduce-scatter.2.cloned.1.call-update
  238.1 215.1 %reduce-scatter.2.cloned.1.call-done = bf16[8,512]{1,0:T(8,128)(2,1)} async-done(((bf16[256,512]{1,0:T(8,128)(2,1)}), bf16[8,512]{1,0:T(8,128)(2,1)}) %reduce-scatter.2.cloned.1.call-update) | async-done | bytes 8208 | tf_op jit(solution)/shard_map/reduce_scatter | solution.py:50
  453.2 1.4 reshape.112
  (13 shorter events, 0.0 us)
Async XLA Ops:
  6.5 83.5 %copy-start = (bf16[896,512]{1,0:T(8,128)(2,1)S(1)}, bf16[896,512]{1,0:T(8,128)(2,1)}, u32[]{:S(2)}) copy-start(bf16[896,512]{1,0:T(8,128)(2,1)} %param.8) | copy-start | bytes 2752516
  6.5 109.5 %copy-start.1 = (bf16[896,512]{1,0:T(8,128)(2,1)S(1)}, bf16[896,512]{1,0:T(8,128)(2,1)}, u32[]{:S(2)}) copy-start(bf16[896,512]{1,0:T(8,128)(2,1)} %param.9) | copy-start | bytes 2752516
  6.5 144.8 %all-gather.2.cloned.1.call-start = ((), (), s32[]{:S(2)}) async-start(), calls=%async_computation.1 | async-start | bytes 15138816 | tf_op jit(solution)/shard_map/all_gather | solution.py:23
  7.3 227.6 %all-reduce.3.cloned.1.call-start = ((), (), s32[]{:S(2)}) async-start(), calls=%async_computation.3 | async-start | bytes 917504 | tf_op jit(solution)/shard_map/psum | solution.py:32
  7.3 13.0 %collective-permute-start = (bf16[896,512]{1,0:T(8,128)(2,1)}, bf16[896,512]{1,0:T(8,128)(2,1)S(1)}, u32[]{:S(2)}, u32[]{:S(2)}) collective-permute-start(bf16[896,512]{1,0:T(8,128)(2,1)} %param.9), channel_id=1, source_target_pairs={{0,1},{1,2},{2,3},{3,4},{4,5},{5,6},{6,7},{7,0},{8,9},{9,10},{10,1... | collective-permute-start | bytes 2752520 | tf_op jit(solution)/shard_map/ppermute | solution.py:11
  20.3 12.8 %collective-permute-start.1 = (bf16[896,512]{1,0:T(8,128)(2,1)S(1)}, bf16[896,512]{1,0:T(8,128)(2,1)S(1)}, u32[]{:S(2)}, u32[]{:S(2)}) collective-permute-start(bf16[896,512]{1,0:T(8,128)(2,1)S(1)} %collective-permute-done), channel_id=1, source_target_pairs={{0,1},{1,2},{2,3},{3,4},{4,5},{5,6},{6,7},{7,0},{8,9},{9,10},{10,1... | collective-permute-start | bytes 2752520 | tf_op jit(solution)/shard_map/ppermute | solution.py:11
  33.2 1.0 copy-start.2
  34.2 12.8 %collective-permute-start.2 = (bf16[896,512]{1,0:T(8,128)(2,1)S(1)}, bf16[896,512]{1,0:T(8,128)(2,1)S(1)}, u32[]{:S(2)}, u32[]{:S(2)}) collective-permute-start(bf16[896,512]{1,0:T(8,128)(2,1)S(1)} %collective-permute-done.1), channel_id=1, source_target_pairs={{0,1},{1,2},{2,3},{3,4},{4,5},{5,6},{6,7},{7,0},{8,9},{9,10},{10,1... | collective-permute-start | bytes 2752520 | tf_op jit(solution)/shard_map/ppermute | solution.py:11
  47.0 0.9 copy-start.4
  47.9 12.8 %collective-permute-start.3 = (bf16[896,512]{1,0:T(8,128)(2,1)S(1)}, bf16[896,512]{1,0:T(8,128)(2,1)S(1)}, u32[]{:S(2)}, u32[]{:S(2)}) collective-permute-start(bf16[896,512]{1,0:T(8,128)(2,1)S(1)} %collective-permute-done.2), channel_id=1, source_target_pairs={{0,1},{1,2},{2,3},{3,4},{4,5},{5,6},{6,7},{7,0},{8,9},{9,10},{10,1... | collective-permute-start | bytes 2752520 | tf_op jit(solution)/shard_map/ppermute | solution.py:11
  60.7 0.9 copy-start.6
  61.7 12.8 %collective-permute-start.4 = (bf16[896,512]{1,0:T(8,128)(2,1)S(1)}, bf16[896,512]{1,0:T(8,128)(2,1)S(1)}, u32[]{:S(2)}, u32[]{:S(2)}) collective-permute-start(bf16[896,512]{1,0:T(8,128)(2,1)S(1)} %collective-permute-done.3), channel_id=1, source_target_pairs={{0,1},{1,2},{2,3},{3,4},{4,5},{5,6},{6,7},{7,0},{8,9},{9,10},{10,1... | collective-permute-start | bytes 2752520 | tf_op jit(solution)/shard_map/ppermute | solution.py:11
  74.5 0.9 copy-start.8
  75.4 12.9 %collective-permute-start.5 = (bf16[896,512]{1,0:T(8,128)(2,1)S(1)}, bf16[896,512]{1,0:T(8,128)(2,1)}, u32[]{:S(2)}, u32[]{:S(2)}) collective-permute-start(bf16[896,512]{1,0:T(8,128)(2,1)S(1)} %collective-permute-done.4), channel_id=1, source_target_pairs={{0,1},{1,2},{2,3},{3,4},{4,5},{5,6},{6,7},{7,0},{8,9},{9,10},{10,1... | collective-permute-start | bytes 2752520 | tf_op jit(solution)/shard_map/ppermute | solution.py:11
  88.4 13.1 %collective-permute-start.6 = (bf16[896,512]{1,0:T(8,128)(2,1)}, bf16[896,512]{1,0:T(8,128)(2,1)}, u32[]{:S(2)}, u32[]{:S(2)}) collective-permute-start(bf16[896,512]{1,0:T(8,128)(2,1)} %collective-permute-done.5), channel_id=1, source_target_pairs={{0,1},{1,2},{2,3},{3,4},{4,5},{5,6},{6,7},{7,0},{8,9},{9,10},{10,1... | collective-permute-start | bytes 2752520 | tf_op jit(solution)/shard_map/ppermute | solution.py:11
  89.2 32.4 %copy-start.9 = (bf16[896,512]{1,0:T(8,128)(2,1)S(1)}, bf16[896,512]{1,0:T(8,128)(2,1)}, u32[]{:S(2)}) copy-start(bf16[896,512]{1,0:T(8,128)(2,1)} %copy-done.8) | copy-start | bytes 2752516
  89.2 33.5 %copy-start.7 = (bf16[896,512]{1,0:T(8,128)(2,1)S(1)}, bf16[896,512]{1,0:T(8,128)(2,1)}, u32[]{:S(2)}) copy-start(bf16[896,512]{1,0:T(8,128)(2,1)} %copy-done.6) | copy-start | bytes 2752516
  89.2 34.5 %copy-start.5 = (bf16[896,512]{1,0:T(8,128)(2,1)S(1)}, bf16[896,512]{1,0:T(8,128)(2,1)}, u32[]{:S(2)}) copy-start(bf16[896,512]{1,0:T(8,128)(2,1)} %copy-done.4) | copy-start | bytes 2752516
  89.2 35.5 %copy-start.3 = (bf16[896,512]{1,0:T(8,128)(2,1)S(1)}, bf16[896,512]{1,0:T(8,128)(2,1)}, u32[]{:S(2)}) copy-start(bf16[896,512]{1,0:T(8,128)(2,1)} %copy-done.2) | copy-start | bytes 2752516
  92.3 59.1 %copy-start.10 = (bf16[1792,64]{0,1:T(8,128)(2,1)S(1)}, bf16[1792,64]{0,1:T(8,128)(2,1)}, u32[]{:S(2)}) copy-start(bf16[1792,64]{0,1:T(8,128)(2,1)} %param.13) | copy-start | bytes 688132
  127.8 46.4 %copy-start.12 = (s32[1,8]{1,0:T(1,128)S(1)}, s32[1,8]{1,0:T(1,128)}, u32[]{:S(2)}) copy-start(s32[1,8]{1,0:T(1,128)} %param.14) | copy-start | bytes 100
  127.8 46.4 %copy-start.11 = (s32[256]{0:T(256)S(1)}, s32[256]{0:T(256)}, u32[]{:S(2)}) copy-start(s32[256]{0:T(256)} %param.15) | copy-start | bytes 3076
  174.1 279.1 %reduce-scatter.2.cloned.1.call-start = ((), (), s32[]{:S(2)}) async-start(), calls=%async_computation.2 | async-start | bytes 270336 | tf_op jit(solution)/shard_map/reduce_scatter | solution.py:50
Sparse Core Ops, SparseCore 0:
  9.8 141.4 all-gather.1
  174.2 60.5 all-reduce.2
  239.2 213.9 reduce-scatter.1
